TPU v7x, 768 devices: a whole 4x8x12 slice. The times are simulated.
768 devices in a mesh: dp: 32 (over y, x), expert: 12 (over z), tensor: 2 (over core).
Axes of the slice: x: 4, y: 8, z: 12, core: 2. Of those that a mesh axis runs over, the one named last changes fastest.
Arguments:
- tokens: bfloat16 [98304, 4096], P(('dp', 'expert'), 'tensor'), may hold values from -6 to 6
- cotangent: bfloat16 [98304, 4096], P(('dp', 'expert'), 'tensor'), may hold values from -0.099609375 to 0.099609375
- latent_down: bfloat16 [4096, 1024], P('tensor'), may hold values from -0.09375 to 0.09375
- latent_up: bfloat16 [1024, 4096], P(None, 'tensor'), may hold values from -0.1875 to 0.1875
- expert_up: bfloat16 [24, 1024, 512], P(('expert', 'tensor')), may hold values from -0.1875 to 0.1875
- expert_down: bfloat16 [24, 512, 1024], P(('expert', 'tensor')), may hold values from -0.25 to 0.25
- routes: int32 [98304, 2], P(('dp', 'expert', 'tensor')), may hold values from 0 to 23, all different within a row; in each aligned block of 128 rows (0 to 127, 128 to 255, ...) at most 16 rows name the same one
- combine: float32 [98304, 2], P(('dp', 'expert', 'tensor')), may hold values from 0.2 to 1
Outputs:
- grad_up: float32 [24, 1024, 512], P(('expert', 'tensor'), 'dp')
- grad_down: float32 [24, 512, 1024], P(('expert', 'tensor'), 'dp')
Inputs may be any that keep to these rules, and one draw needn't show every extreme that they name: `routes`: each token names 2 different experts. The 128 tokens of one device name no expert in more than 16 slots, and in every draw some device names some expert in exactly 16 slots.
All inputs are finite; a program needn't handle non-finite values.
Results may differ from a plain program's by a relative error of at most 0.025.
Values may be sent and summed in bfloat16 or wider, within the bound.
A program may use at most 64 MiB of HBM per device.

v0:
```python
import jax
import jax.numpy as jnp
from jax import lax
from jax.sharding import PartitionSpec as P


def shards(tokens, cotangent, latent_down, latent_up, expert_up, expert_down, routes, combine):
    tensor_size = lax.axis_size("tensor")
    expert_size = lax.axis_size("expert")
    latent_width = latent_down.shape[1]
    tok_dev = routes.shape[0]
    top_count = routes.shape[1]
    expert_count = expert_size * tensor_size
    capacity = max(2, 3 * tok_dev * top_count // (2 * expert_count))
    forward_part = jnp.dot(tokens, latent_down, preferred_element_type=jnp.float32)
    backward_part = lax.dot_general(
        cotangent, latent_up, (((1,), (1,)), ((), ())), preferred_element_type=jnp.float32
    )
    summed = lax.psum_scatter(
        jnp.concatenate([forward_part, backward_part], axis=1).astype(jnp.bfloat16),
        "tensor",
        scatter_dimension=0,
        tiled=True,
    ).astype(jnp.float32)
    latent = summed[:, :latent_width].astype(jnp.bfloat16)
    back_latent = summed[:, latent_width:]
    slot_grad = (combine[:, :, None] * back_latent[:, None, :]).astype(jnp.bfloat16)
    latent_rep = jnp.broadcast_to(latent[:, None, :], (tok_dev, top_count, latent_width))
    payload = jnp.concatenate([latent_rep, slot_grad], axis=2).reshape(
        tok_dev * top_count, 2 * latent_width
    )
    chosen = routes.reshape(-1)
    onehot = (chosen[:, None] == jnp.arange(expert_count, dtype=jnp.int32)[None, :]).astype(
        jnp.int32
    )
    slot_rank = jnp.sum(onehot * (jnp.cumsum(onehot, axis=0) - 1), axis=1)
    target = (
        chosen % tensor_size * (expert_size * capacity)
        + chosen // tensor_size * capacity
        + slot_rank
    )
    outgoing = jnp.zeros((tensor_size * expert_size * capacity, 2 * latent_width), jnp.bfloat16)
    outgoing = outgoing.at[target].set(payload)
    outgoing = outgoing.reshape(tensor_size, expert_size, capacity, 2 * latent_width)
    halfway = lax.all_to_all(outgoing, "tensor", split_axis=0, concat_axis=0, tiled=True)
    arrived = lax.all_to_all(halfway, "expert", split_axis=1, concat_axis=1, tiled=True)
    slot_rows = arrived.reshape(-1, 2 * latent_width)
    lat_rows = slot_rows[:, :latent_width]
    grad_rows = slot_rows[:, latent_width:]
    weight_up = expert_up[0]
    weight_down = expert_down[0]
    pre = jnp.dot(lat_rows, weight_up, preferred_element_type=jnp.float32)
    positive = jnp.maximum(pre, 0.0)
    act = (positive * positive).astype(jnp.bfloat16)
    part_down = lax.dot_general(
        act, grad_rows, (((0,), (0,)), ((), ())), preferred_element_type=jnp.float32
    )
    hidden_grad = lax.dot_general(
        grad_rows, weight_down, (((1,), (1,)), ((), ())), preferred_element_type=jnp.float32
    )
    pre_grad = (hidden_grad * 2.0 * positive).astype(jnp.bfloat16)
    part_up = lax.dot_general(
        lat_rows, pre_grad, (((0,), (0,)), ((), ())), preferred_element_type=jnp.float32
    )
    grad_up, grad_down = (
        lax.psum_scatter(
            part_up[None].astype(jnp.bfloat16), "dp", scatter_dimension=1, tiled=True
        ).astype(jnp.float32),
        lax.psum_scatter(
            part_down[None].astype(jnp.bfloat16), "dp", scatter_dimension=1, tiled=True
        ).astype(jnp.float32),
    )
    return (grad_up, grad_down)


def solution(mesh):
    return jax.shard_map(
        shards,
        mesh=mesh,
        in_specs=(
            P(("dp", "expert"), "tensor"),
            P(("dp", "expert"), "tensor"),
            P("tensor", None),
            P(None, "tensor"),
            P(("expert", "tensor"), None, None),
            P(("expert", "tensor"), None, None),
            P(("dp", "expert", "tensor"), None),
            P(("dp", "expert", "tensor"), None),
        ),
        out_specs=(P(("expert", "tensor"), "dp", None), P(("expert", "tensor"), "dp", None)),
        check_vma=False,
    )
```

profile of v0, /device:TPU:1, one launch (start us, length us, event | category | flops | bytes accessed | tf_op | source)
XLA Modules:
  0.0 576.4 jit_solution(6392525783246100226)
XLA Ops:
  7.2 3.9 convolution_convert_fusion.2
  11.3 1.3 convolution_convert_fusion.3
  12.7 1.1 pad_maximum_fusion
  14.4 0.6 reduce-window.6
  15.0 0.2 slice_reduce_fusion
  15.6 27.5 %reduce-scatter.4.cloned.1.call-done = bf16[128,2048]{1,0:T(8,128)(2,1)} async-done(((bf16[256,2048]{1,0:T(8,128)(2,1)}), bf16[128,2048]{1,0:T(8,128)(2,1)}) %reduce-scatter.4.cloned.1.call-update) | async-done | bytes 524304 | tf_op jit(solution)/shard_map/reduce_scatter | solution.py:19
  43.1 1.1 fusion.26
  44.2 0.4 mul.66
  44.5 0.7 mul.67
  45.3 0.3 broadcast_in_dim.5
  45.6 0.2 concatenate.11
  45.8 0.9 multiply_convert_fusion
  46.7 3.1 scatter_custom_fusion
  49.8 4.6 all_to_all.10
  54.6 64.3 %all_to_all.11 = bf16[2,12,16,2048]{3,2,0,1:T(8,128)(2,1)S(1)} all-to-all(bf16[2,12,16,2048]{3,2,0,1:T(8,128)(2,1)S(1)} %copy.25), channel_id=1, replica_groups=mesh['dp'=32,'expert'=12,'tensor'=2] {'expert'}, dimensions={1} | all-to-all | bytes 3145728 | tf_op jit(solution)/shard_map/all_to_all | solution.py:46
  118.9 0.2 copy.26
  119.1 1.1 copy-done.5
  120.1 0.6 convolution_maximum_fusion
  120.7 1.8 fusion.1
  122.6 2.3 fusion
  124.9 214.4 %reduce-scatter.8.cloned.1.call-done = bf16[1,16,1024]{2,1,0:T(8,128)(2,1)} async-done(((bf16[1,512,1024]{2,1,0:T(8,128)(2,1)}), bf16[1,16,1024]{2,1,0:T(8,128)(2,1)}) %reduce-scatter.8.cloned.1.call-update) | async-done | bytes 32784 | tf_op jit(solution)/shard_map/reduce_scatter | solution.py:69
  339.3 1.4 convert_element_type.45
  340.7 227.8 %reduce-scatter.6.cloned.1.call-done = bf16[1,32,512]{2,1,0:T(8,128)(2,1)} async-done(((bf16[1,1024,512]{2,1,0:T(8,128)(2,1)}), bf16[1,32,512]{2,1,0:T(8,128)(2,1)}) %reduce-scatter.6.cloned.1.call-update) | async-done | bytes 32784 | tf_op jit(solution)/shard_map/reduce_scatter | solution.py:66
  568.5 1.4 convert_element_type.41
  (29 shorter events, 1.4 us)
Async XLA Ops:
  7.2 115.4 %copy-start = (bf16[1,512,1024]{2,1,0:T(8,128)(2,1)S(1)}, bf16[1,512,1024]{2,1,0:T(8,128)(2,1)}, u32[]{:S(2)}) copy-start(bf16[1,512,1024]{2,1,0:T(8,128)(2,1)} %param.13) | copy-start | bytes 3145732
  7.2 4.0 copy-start.4
  7.2 35.9 %reduce-scatter.4.cloned.1.call-start = ((), (), s32[]{:S(2)}) async-start(), calls=%async_computation.5 | async-start | bytes 1572864 | tf_op jit(solution)/shard_map/reduce_scatter | solution.py:19
  7.2 4.1 copy-start.3
  12.6 1.2 copy-start.1
  12.6 2.6 copy-start.2
  13.8 325.5 %reduce-scatter.8.cloned.1.call-start = ((), (), s32[]{:S(2)}) async-start(), calls=%async_computation.7 | async-start | bytes 1081344 | tf_op jit(solution)/shard_map/reduce_scatter | solution.py:69
  118.9 1.2 copy-start.5
  122.5 445.9 %reduce-scatter.6.cloned.1.call-start = ((), (), s32[]{:S(2)}) async-start(), calls=%async_computation.6 | async-start | bytes 1081344 | tf_op jit(solution)/shard_map/reduce_scatter | solution.py:66
Sparse Core Ops, SparseCore 0:
  13.9 29.1 reduce-scatter.3
  122.6 216.5 reduce-scatter.7
  345.0 223.3 reduce-scatter.5
where the time goes:
time: 581 us; the launch traced here: 576 us
  waiting for transfers between devices  470 us (81%)
  blocking collectives  68.9 us (12%)
  between operations  13.9 us (2%)
  matrix products  9.83 us (2%)
  other arithmetic  9.72 us (2%)
    reduce_scatter x1, waiting for transfers between devices, shards(): lax.psum_scatter(part_up[None].astype(jnp.bfloat16), 'dp', scatter_dimens...  228 us
    reduce_scatter x1, waiting for transfers between devices, shards(): lax.psum_scatter(part_down[None].astype(jnp.bfloat16), 'dp', scatter_dime...  214 us
    all_to_all x1, blocking collectives, shards(): lax.all_to_all(halfway, 'expert', split_axis=1, concat_axis=1, tiled=True)  64.3 us
    reduce_scatter x1, waiting for transfers between devices, shards(): lax.psum_scatter(jnp.concatenate([forward_part, backward_part], axis=1).a...  27.5 us
  transfers between devices with their start and end apart: 3, of which 3 were waited for; matrix products, arithmetic and copies ran while one was open for 1% of the time, Pallas kernels for 0%

commit v1 on v0

v1 whole, which is shorter than its diff:
```python
import functools

import jax
import jax.numpy as jnp
from jax import lax
from jax.experimental import pallas as pl
from jax.experimental.pallas import tpu as pltpu
from jax.sharding import PartitionSpec as P

F32 = jnp.float32
BF16 = jnp.bfloat16
MESH = pl.DeviceIdType.MESH
NY, NX = 8, 4


def remote(src, dst, send_sem, recv_sem, device):
    return pltpu.make_async_remote_copy(
        src_ref=src,
        dst_ref=dst,
        send_sem=send_sem,
        recv_sem=recv_sem,
        device_id=device,
        device_id_type=MESH,
    )


def dot(a, b, dims=((1,), (0,))):
    return lax.dot_general(a, b, (dims, ((), ())), preferred_element_type=F32)


class RingSum:
    def __init__(self, chunk, land, send_sem, recv_sem, me, n, device):
        self.chunk, self.land = chunk, land
        self.send_sem, self.recv_sem = send_sem, recv_sem
        self.me, self.n, self.half, self.device = me, n, n // 2, device
        self.m = chunk.shape[1]
        self.sent = []

    def part(self, way):
        h = self.m // 2
        return pl.ds(0, h) if way == 0 else pl.ds(h, h)

    def owner(self, way, distance):
        if way == 0:
            return lax.rem(self.me + distance, self.n)
        return lax.rem(self.me + self.n - distance, self.n)

    def copy(self, way, step):
        src = self.chunk.at[self.owner(way, self.half - step)]
        if step == 0:
            src = src.at[self.part(way)]
            dst = self.land.at[way, 0, self.part(way)]
        else:
            dst = self.land.at[way, step]
        return remote(
            src,
            dst,
            self.send_sem.at[way, step],
            self.recv_sem.at[way, step],
            self.device(self.owner(way, 1)),
        )

    def start(self, step):
        for way in (0, 1):
            if step > 0:
                self.copy(way, step - 1).wait_recv()
                target = self.owner(way, self.half - step)
                piece = self.part(way) if step == 1 else pl.ds(0, self.m)
                total = self.chunk[target, piece].astype(F32) + self.land[
                    way, step - 1, piece
                ].astype(F32)
                self.chunk[target, piece] = total.astype(BF16)
            copy = self.copy(way, step)
            copy.start()
            self.sent.append(copy)

    def finish(self):
        step = self.half - 1
        for way in (0, 1):
            self.copy(way, step).wait_recv()
        own = self.chunk[self.me].astype(F32)
        if self.half == 1:
            return own + self.last_halves()
        return own + self.land[0, step].astype(F32) + self.land[1, step].astype(F32)

    def last_halves(self):
        h = self.m // 2
        return jnp.concatenate([self.land[0, 0, :h], self.land[1, 0, h:]], axis=0).astype(F32)


def layer(
    ny, nx, nz, cap,
    tok_hbm, cot_hbm, down_hbm, up_hbm, wup_hbm, wdn_hbm, routes_ref, combine_ref,
    gup_ref, gdn_ref,
    tok, cot, down, up, wup, wdn, load_sem,
    part_f, part_b, got_f, got_b, swap_send, swap_recv,
    out_lat, out_grad, in_lat, in_grad, a2a_send, a2a_recv, own_sem,
    act_ref, pre_grad_ref,
    chunk_a, chunk_b, land_a, land_b, ring_a_send, ring_a_recv, ring_b_send, ring_b_recv,
    next_a, next_b, got_a, got_b2, dir_a_send, dir_a_recv, dir_b_send, dir_b_recv,
):
    group = lax.axis_index("dp")
    z = lax.axis_index("expert")
    core = lax.axis_index("tensor")
    other = 1 - core
    y, x = group // nx, lax.rem(group, nx)
    tok_dev = routes_ref.shape[1]
    width = down.shape[1]
    experts = 2 * nz

    def at_x(xx):
        return {"dp": y * nx + xx}

    def at_y(yy):
        return {"dp": yy * nx + x}

    loads = [
        pltpu.make_async_copy(src, dst, load_sem.at[i])
        for i, (src, dst) in enumerate(
            [(tok_hbm, tok), (down_hbm, down), (cot_hbm, cot), (up_hbm, up), (wup_hbm.at[0], wup), (wdn_hbm.at[0], wdn)]
        )
    ]
    for load in loads:
        load.start()

    barrier = pltpu.get_barrier_semaphore()

    def greet(device):
        pl.semaphore_signal(barrier, inc=1, device_id=device, device_id_type=MESH)

    greet({"tensor": other})
    for k in range(1, nz):
        for cc in range(2):
            greet({"expert": lax.rem(z + k, nz), "tensor": cc})
    for k in range(1, nx):
        greet(at_x(lax.rem(x + k, nx)))
    for k in range(1, ny):
        greet(at_y(lax.rem(y + k, ny)))

    step = min(256, width)
    loads[0].wait()
    loads[1].wait()
    for j in range(0, width, step):
        part_f[:, j : j + step] = dot(tok[...], down[:, j : j + step]).astype(BF16)
    pl.semaphore_wait(barrier, 1 + 2 * (nz - 1) + (nx - 1) + (ny - 1))
    theirs = pl.ds(pl.multiple_of(other * tok_dev, tok_dev), tok_dev)
    mine = pl.ds(pl.multiple_of(core * tok_dev, tok_dev), tok_dev)
    swap_f = remote(part_f.at[theirs], got_f, swap_send.at[0], swap_recv.at[0], {"tensor": other})
    swap_f.start()
    loads[2].wait()
    loads[3].wait()
    for j in range(0, width, step):
        part_b[:, j : j + step] = dot(cot[...], up[j : j + step, :], ((1,), (1,))).astype(BF16)
    swap_b = remote(part_b.at[theirs], got_b, swap_send.at[1], swap_recv.at[1], {"tensor": other})
    swap_b.start()

    before = (
        lax.broadcasted_iota(jnp.int32, (tok_dev, tok_dev), 0)
        < lax.broadcasted_iota(jnp.int32, (tok_dev, tok_dev), 1)
    ).astype(BF16)
    expert_id = lax.broadcasted_iota(jnp.int32, (experts, tok_dev), 0)
    slot_id = lax.broadcasted_iota(jnp.int32, (experts * cap, tok_dev), 0)
    taken = jnp.zeros((experts, 1), F32)
    table = jnp.zeros((experts * cap, tok_dev), F32)
    weight = jnp.zeros((experts * cap, 1), F32)
    for k in range(routes_ref.shape[0]):
        chosen = routes_ref[k : k + 1, :]
        named = (expert_id == chosen).astype(F32)
        count = dot(named.astype(BF16), before) + taken
        rank = jnp.sum(named * count, axis=0, keepdims=True)
        taken = taken + jnp.sum(named, axis=1, keepdims=True)
        here = slot_id == chosen * cap + rank.astype(jnp.int32)
        table = table + here.astype(F32)
        weight = weight + jnp.sum(
            jnp.where(here, combine_ref[k : k + 1, :], 0.0), axis=1, keepdims=True
        )
    table = table.astype(BF16)

    order = sorted(range(1, nz), key=lambda k: -min(k, nz - k))
    sent = []

    def dispatch(which, outgoing, incoming):
        for k in order:
            zz = lax.rem(z + k, nz)
            for cc in range(2):
                copy = remote(
                    outgoing.at[2 * zz + cc],
                    incoming.at[2 * k + core],
                    a2a_send.at[which, 2 * k + cc],
                    a2a_recv.at[which, 2 * k + core],
                    {"expert": zz, "tensor": cc},
                )
                copy.start()
                sent.append(copy)
        copy = remote(
            outgoing.at[2 * z + other],
            incoming.at[core],
            a2a_send.at[which, other],
            a2a_recv.at[which, core],
            {"tensor": other},
        )
        copy.start()
        sent.append(copy)
        own = pltpu.make_async_copy(
            outgoing.at[2 * z + core], incoming.at[core], own_sem.at[which]
        )
        own.start()
        return own

    def collect(which, incoming, own):
        for k in reversed(order):
            for cc in range(2):
                remote(
                    incoming.at[2 * k + cc],
                    incoming.at[2 * k + cc],
                    a2a_send.at[which, 2 * k + cc],
                    a2a_recv.at[which, 2 * k + cc],
                    {"expert": lax.rem(z + k, nz), "tensor": cc},
                ).wait_recv()
        remote(
            incoming.at[other],
            incoming.at[other],
            a2a_send.at[which, other],
            a2a_recv.at[which, other],
            {"tensor": other},
        ).wait_recv()
        own.wait()

    swap_f.wait_recv()
    lat = (part_f[mine].astype(F32) + got_f[...].astype(F32)).astype(BF16)
    out_lat[...] = dot(table, lat).astype(BF16).reshape(out_lat.shape)
    own_lat = dispatch(0, out_lat, in_lat)
    swap_b.wait_recv()
    back = dot(table, part_b[mine]) + dot(table, got_b[...])
    out_grad[...] = (weight * back).astype(BF16).reshape(out_grad.shape)
    own_grad = dispatch(1, out_grad, in_grad)

    loads[4].wait()
    loads[5].wait()
    collect(0, in_lat, own_lat)
    lat_rows = in_lat[...].reshape(-1, width)
    positive = jnp.maximum(dot(lat_rows, wup[...]), 0.0)
    act_ref[...] = (positive * positive).astype(BF16)
    collect(1, in_grad, own_grad)
    grad_rows = in_grad[...].reshape(-1, width)
    hidden_grad = dot(grad_rows, wdn[...], ((1,), (1,)))
    pre_grad_ref[...] = (hidden_grad * 2.0 * positive).astype(BF16)

    rows = chunk_a.shape[2]
    for j in range(0, width, step):
        piece = dot(act_ref[...], grad_rows[:, j : j + step], ((0,), (0,)))
        piece = piece.astype(BF16).reshape(ny, nx, rows, step)
        for xx in range(nx):
            chunk_a[xx, :, :, j : j + step] = piece[:, xx]
    ring_a = RingSum(chunk_a, land_a, ring_a_send, ring_a_recv, x, nx, at_x)
    ring_b = RingSum(chunk_b, land_b, ring_b_send, ring_b_recv, y, ny, at_y)
    ring_a.start(0)
    hidden = wup.shape[1]
    step = min(step, hidden)
    for j in range(0, hidden, step):
        piece = dot(lat_rows, pre_grad_ref[:, j : j + step], ((0,), (0,)))
        piece = piece.astype(BF16).reshape(ny, nx, 2, rows, step)
        for half in range(2):
            chunk_b[:, :, :, half * hidden + j : half * hidden + j + step] = piece[:, :, half]
    ring_b.start(0)
    ring_a.start(1)
    ring_b.start(1)
    ring_b.start(2)
    sum_a = ring_a.finish()
    next_a[...] = sum_a.astype(BF16)

    def spread(source, land, send_sem, recv_sem, me, n, device):
        copies = []
        for k in range(1, n):
            target = lax.rem(me + k, n)
            copy = remote(source.at[target], land.at[k], send_sem.at[k], recv_sem.at[k], device(target))
            copy.start()
            copies.append(copy)
        return copies

    def total(source, land, copies, me):
        out = source[me].astype(F32)
        for k, copy in enumerate(copies, 1):
            copy.wait_recv()
            out = out + land[k].astype(F32)
        return out

    spread_a = spread(next_a, got_a, dir_a_send, dir_a_recv, y, ny, at_y)
    ring_b.start(3)
    next_b[...] = ring_b.finish().astype(BF16)
    spread_b = spread(next_b, got_b2, dir_b_send, dir_b_recv, x, nx, at_x)
    gdn_ref[0] = total(next_a, got_a, spread_a, y)
    sum_b = total(next_b, got_b2, spread_b, x)
    gup_ref[0, 0:rows, :] = sum_b[:, :hidden]
    gup_ref[0, rows : 2 * rows, :] = sum_b[:, hidden:]

    for copy in [swap_f, swap_b] + sent + ring_a.sent + ring_b.sent + spread_a + spread_b:
        copy.wait_send()


def shards(ny, nx, tokens, cotangent, latent_down, latent_up, expert_up, expert_down, routes, combine):
    nz = lax.axis_size("expert")
    tok_dev, top = routes.shape
    width, hidden = expert_up.shape[1:]
    experts = 2 * nz
    cap = max(2, 3 * tok_dev * top // (2 * experts))
    rows = hidden // (ny * nx)
    assert width == 2 * hidden

    def sems(*shape):
        return pltpu.SemaphoreType.DMA(shape)

    vmem = pltpu.VMEM
    any_spec = pl.BlockSpec(memory_space=pl.ANY)
    vmem_spec = pl.BlockSpec(memory_space=pltpu.VMEM)
    return pl.pallas_call(
        functools.partial(layer, ny, nx, nz, cap),
        out_shape=(
            jax.ShapeDtypeStruct((1, width // (ny * nx), hidden), F32),
            jax.ShapeDtypeStruct((1, rows, width), F32),
        ),
        in_specs=[any_spec] * 6 + [vmem_spec] * 2,
        out_specs=(vmem_spec, vmem_spec),
        scratch_shapes=[
            vmem(tokens.shape, BF16), vmem(cotangent.shape, BF16),
            vmem(latent_down.shape, BF16), vmem(latent_up.shape, BF16),
            vmem((width, hidden), BF16), vmem((hidden, width), BF16), sems(6),
            vmem((2 * tok_dev, width), BF16), vmem((2 * tok_dev, width), BF16),
            vmem((tok_dev, width), BF16), vmem((tok_dev, width), BF16), sems(2), sems(2),
            vmem((experts, cap, width), BF16), vmem((experts, cap, width), BF16),
            vmem((experts, cap, width), BF16), vmem((experts, cap, width), BF16),
            sems(2, experts), sems(2, experts), sems(2),
            vmem((experts * cap, hidden), BF16), vmem((experts * cap, hidden), BF16),
            vmem((nx, ny, rows, width), BF16), vmem((ny, nx, rows, width), BF16),
            vmem((2, nx // 2, ny, rows, width), BF16), vmem((2, ny // 2, nx, rows, width), BF16),
            sems(2, nx // 2), sems(2, nx // 2), sems(2, ny // 2), sems(2, ny // 2),
            vmem((ny, rows, width), BF16), vmem((nx, rows, width), BF16),
            vmem((ny, rows, width), BF16), vmem((nx, rows, width), BF16),
            sems(ny), sems(ny), sems(nx), sems(nx),
        ],
        compiler_params=pltpu.CompilerParams(
            collective_id=0, has_side_effects=True, vmem_limit_bytes=56 * 1024 * 1024
        ),
        cost_estimate=pl.CostEstimate(flops=4 * 10**9, bytes_accessed=13 * 10**6, transcendentals=0),
    )(tokens, cotangent, latent_down, latent_up, expert_up, expert_down, routes.T, combine.T)


def solution(mesh):
    return jax.shard_map(
        functools.partial(shards, NY, NX),
        mesh=mesh,
        in_specs=(
            P(("dp", "expert"), "tensor"),
            P(("dp", "expert"), "tensor"),
            P("tensor", None),
            P(None, "tensor"),
            P(("expert", "tensor"), None, None),
            P(("expert", "tensor"), None, None),
            P(("dp", "expert", "tensor"), None),
            P(("dp", "expert", "tensor"), None),
        ),
        out_specs=(P(("expert", "tensor"), "dp", None), P(("expert", "tensor"), "dp", None)),
        check_vma=False,
    )
```

time: 581 us -> 108 us (0.19)
  waiting for transfers between devices: 470 us -> 0 us
  Pallas kernels: 0 us -> 104 us
  blocking collectives: 68.9 us -> 0 us
  between operations: 13.9 us -> 0.64 us
  matrix products: 9.83 us -> 0 us
  other arithmetic: 9.72 us -> 0 us
    reduce_scatter x3 -> x0, waiting for transfers between devices: 470 us -> none  [the longest x1 228 us: shards(): lax.psum_scatter(part_up[None].astype(jnp.bfloat16), 'dp', scatter_dimens...]
    pallas_call x0 -> x1, Pallas kernels: none -> 104 us  [shards(): pl.pallas_call(functools.partial(layer, ny, nx, nz, cap), out_shape=(jax....]
    all_to_all x2 -> x0, blocking collectives: 68.9 us -> none  [the longest x1 64.3 us: shards(): lax.all_to_all(halfway, 'expert', split_axis=1, concat_axis=1, tiled=True)]
    dot_general x5 -> x0, matrix products: 9.83 us -> none  [the longest x1 3.93 us: shards(): lax.dot_general(cotangent, latent_up, (((1,), (1,)), ((), ())), preferred...]
  transfers between devices with their start and end apart: 3 -> 0, of which waited for: 3 -> 0; matrix products, arithmetic and copies ran while one was open for 1% -> 0% of each run, Pallas kernels for 0% -> 0%
where the time goes in v1:
time: 108 us
  Pallas kernels  104 us (96%)
  local copies, waits for them, and re-layouts  2.95 us (3%)
    pallas_call x1, Pallas kernels, shards(): pl.pallas_call(functools.partial(layer, ny, nx, nz, cap), out_shape=(jax....  104 us
    unnamed x2, local copies, waits for them, and re-layouts  2.95 us

profile of v1, /device:TPU:1, one launch (start us, length us, event | category | flops | bytes accessed | tf_op | source)
XLA Modules:
  0.0 107.6 jit_solution(8503344630989442839)
XLA Ops:
  0.6 104.0 %shard_map.95 = (f32[1,32,512]{2,1,0:T(8,128)}, f32[1,16,1024]{2,1,0:T(8,128)}) custom-call(bf16[256,2048]{1,0:T(8,128)(2,1)} %tok_hbm.1, bf16[256,2048]{1,0:T(8,128)(2,1)} %cot_hbm.1, bf16[2048,1024]{1,0:T(8,128)(2,1)} %down_hbm.1, bf16[1024,2048]{1,0:T(8,128)(2,1)} %up_hbm.1, bf16[1,1024,512]{2,1,0:T(8,128)(2,1)} %wup_hbm.1, ...), custom_call_target="tpu_custom_call" | custom-call | flops 4000000000 | bytes 13000000 | tf_op jit(solution)/shard_map/pallas_call | solution.py:316
  104.6 1.5 %copy.12 = f32[1,32,512]{2,1,0:T(8,128)} copy(f32[1,32,512]{2,1,0:T(8,128)} %get-tuple-element.4) | data formatting | bytes 131072
  106.1 1.5 %copy.13 = f32[1,16,1024]{2,1,0:T(8,128)} copy(f32[1,16,1024]{2,1,0:T(8,128)} %get-tuple-element.5) | data formatting | bytes 131072

commit v2 on v1

v2 whole, which is shorter than its diff:
```python
import functools

import jax
import jax.numpy as jnp
from jax import lax
from jax.experimental import pallas as pl
from jax.experimental.pallas import tpu as pltpu
from jax.sharding import PartitionSpec as P

F32 = jnp.float32
BF16 = jnp.bfloat16
MESH = pl.DeviceIdType.MESH
NY, NX = 8, 4


def remote(src, dst, send_sem, recv_sem, device):
    return pltpu.make_async_remote_copy(
        src_ref=src,
        dst_ref=dst,
        send_sem=send_sem,
        recv_sem=recv_sem,
        device_id=device,
        device_id_type=MESH,
    )


def dot(a, b, dims=((1,), (0,))):
    return lax.dot_general(a, b, (dims, ((), ())), preferred_element_type=F32)


class Direct:
    def __init__(self, source, landing, sems, me, n, device):
        send_sem, recv_sem = sems
        self.sent, self.recv = [], []
        for k in range(1, n):
            target = lax.rem(me + k, n)
            sender = lax.rem(me + n - k, n)
            copy = remote(
                source(target), landing(me, k), send_sem.at[k], recv_sem.at[k], device(target)
            )
            copy.start()
            self.sent.append(copy)
            here = landing(sender, k)
            self.recv.append(remote(here, here, send_sem.at[k], recv_sem.at[k], device(target)))

    def wait(self):
        for copy in self.recv:
            copy.wait_recv()


class Ring:
    def __init__(self, me, n, device):
        self.me, self.n, self.device = me, n, device


class TwoStepSum:
    def __init__(self, refs, first, second):
        self.chunk, self.land, self.next, self.got, send1, recv1, send2, recv2 = refs
        self.first, self.second = first, second
        self.sems1, self.sems2 = (send1, recv1), (send2, recv2)

    def start(self):
        r = self.first
        self.step1 = Direct(
            lambda t: self.chunk.at[t], lambda s, k: self.land.at[k], self.sems1, r.me, r.n, r.device
        )

    def turn(self):
        self.step1.wait()
        total = self.chunk[self.first.me].astype(F32)
        for k in range(1, self.first.n):
            total = total + self.land[k].astype(F32)
        self.next[...] = total.astype(BF16)
        r = self.second
        self.step2 = Direct(
            lambda t: self.next.at[t], lambda s, k: self.got.at[k], self.sems2, r.me, r.n, r.device
        )

    def total(self):
        self.step2.wait()
        total = self.next[self.second.me].astype(F32)
        for k in range(1, self.second.n):
            total = total + self.got[k].astype(F32)
        return total

    def sent(self):
        return self.step1.sent + self.step2.sent


class PlaneSum:
    def __init__(self, refs, xs, ys):
        n = len(refs) // 3
        self.down = TwoStepSum(refs[:n], xs, ys)
        self.up0 = TwoStepSum(refs[n : 2 * n], xs, ys)
        self.up1 = TwoStepSum(refs[2 * n :], ys, xs)

    def sent(self):
        return self.down.sent() + self.up0.sent() + self.up1.sent()


def layer(
    ny, nx, nz, cap,
    tok_hbm, cot_hbm, down_hbm, up_hbm, wup_hbm, wdn_hbm, routes_ref, combine_ref,
    gup_ref, gdn_ref,
    tok, cot, down, up, wup, wdn, load_sem,
    part_f, part_b, got_f, got_b, swap_send, swap_recv,
    out_lat, out_grad, in_lat, in_grad, a2a_send, a2a_recv, own_sem,
    wup2, wdn2, slice_send, slice_recv,
    act_ref, pre_grad_ref, far_out, far_in, far_send, far_recv,
    *more,
):
    group = lax.axis_index("dp")
    z = lax.axis_index("expert")
    core = lax.axis_index("tensor")
    other = 1 - core
    y, x = group // nx, lax.rem(group, nx)
    tok_dev = routes_ref.shape[1]
    width, hidden = wup.shape
    experts = 2 * nz
    far = nz // 2
    reach = nz // 4
    far_z = lax.rem(z + far, nz)

    xs = Ring(x, nx, lambda xx: {"dp": y * nx + xx})
    ys = Ring(y, ny, lambda yy: {"dp": yy * nx + x})

    def plane(j):
        return lax.rem(z + j + nz, nz)

    loads = [
        pltpu.make_async_copy(src, dst, load_sem.at[i])
        for i, (src, dst) in enumerate(
            [(tok_hbm, tok), (down_hbm, down), (cot_hbm, cot), (up_hbm, up), (wup_hbm.at[0], wup), (wdn_hbm.at[0], wdn)]
        )
    ]
    for load in loads:
        load.start()

    barrier = pltpu.get_barrier_semaphore()
    greeted = []

    def greet(device):
        greeted.append(device)
        pl.semaphore_signal(barrier, inc=1, device_id=device, device_id_type=MESH)

    greet({"tensor": other})
    for j in range(1, nz):
        for cc in range(2):
            greet({"expert": plane(j), "tensor": cc})
    for k in range(1, nx):
        greet(xs.device(lax.rem(x + k, nx)))
    for k in range(1, ny):
        greet(ys.device(lax.rem(y + k, ny)))

    step = min(256, width)
    loads[0].wait()
    loads[1].wait()
    for j in range(0, width, step):
        part_f[:, j : j + step] = dot(tok[...], down[:, j : j + step]).astype(BF16)
    pl.semaphore_wait(barrier, len(greeted))
    theirs = pl.ds(pl.multiple_of(other * tok_dev, tok_dev), tok_dev)
    mine = pl.ds(pl.multiple_of(core * tok_dev, tok_dev), tok_dev)
    swap_f = remote(part_f.at[theirs], got_f, swap_send.at[0], swap_recv.at[0], {"tensor": other})
    swap_f.start()

    up_rows, dn_rows = wup2.shape[2], wdn2.shape[2]
    slices = [
        remote(
            wup_hbm.at[0, pl.ds(pl.multiple_of(group * up_rows, up_rows), up_rows)],
            wup2.at[y, x], slice_send.at[0], slice_recv.at[0], {"expert": far_z},
        ),
        remote(
            wdn_hbm.at[0, pl.ds(pl.multiple_of(group * dn_rows, dn_rows), dn_rows)],
            wdn2.at[y, x], slice_send.at[1], slice_recv.at[1], {"expert": far_z},
        ),
    ]

    @pl.when(core == 0)
    def _():
        for copy in slices:
            copy.start()

    loads[2].wait()
    loads[3].wait()
    for j in range(0, width, step):
        part_b[:, j : j + step] = dot(cot[...], up[j : j + step, :], ((1,), (1,))).astype(BF16)
    swap_b = remote(part_b.at[theirs], got_b, swap_send.at[1], swap_recv.at[1], {"tensor": other})
    swap_b.start()

    before = (
        lax.broadcasted_iota(jnp.int32, (tok_dev, tok_dev), 0)
        < lax.broadcasted_iota(jnp.int32, (tok_dev, tok_dev), 1)
    ).astype(BF16)
    expert_id = lax.broadcasted_iota(jnp.int32, (experts, tok_dev), 0)
    slot_id = lax.broadcasted_iota(jnp.int32, (experts * cap, tok_dev), 0)
    taken = jnp.zeros((experts, 1), F32)
    table = jnp.zeros((experts * cap, tok_dev), F32)
    weight = jnp.zeros((experts * cap, 1), F32)
    for k in range(routes_ref.shape[0]):
        chosen = routes_ref[k : k + 1, :]
        named = (expert_id == chosen).astype(F32)
        count = dot(named.astype(BF16), before) + taken
        rank = jnp.sum(named * count, axis=0, keepdims=True)
        taken = taken + jnp.sum(named, axis=1, keepdims=True)
        here = slot_id == chosen * cap + rank.astype(jnp.int32)
        table = table + here.astype(F32)
        weight = weight + jnp.sum(
            jnp.where(here, combine_ref[k : k + 1, :], 0.0), axis=1, keepdims=True
        )
    table = table.astype(BF16)

    second = [(k, k - far) for k in range(nz) if reach < k < nz - reach]
    first = [(k, k if k <= reach else k - nz) for k in range(nz) if k <= reach or k >= nz - reach]
    second_blocks, first_blocks = 2 * len(second), 2 * len(first)

    def places(moves, start):
        low = min(j for _, j in moves)
        return sorted([(k, j, start + 2 * (j - low)) for k, j in moves], key=lambda m: -abs(m[1]))

    second, first = places(second, 0), places(first, second_blocks)
    single = sorted([(k, k, 2 * k) for k in range(nz)], key=lambda m: -min(m[0], nz - m[0]))
    buffers = ((out_lat, in_lat), (out_grad, in_grad))

    def send(which, k, j, base, to, stay):
        outgoing, incoming = buffers[which]
        block = outgoing.at[2 * lax.rem(z + k, nz) + to]
        if stay:
            return pltpu.make_async_copy(block, incoming.at[base + to], own_sem.at[which, 0 if k == 0 else 1])
        return remote(
            block,
            incoming.at[base + core],
            a2a_send.at[which, nz * to + k],
            a2a_recv.at[which, base + core],
            {"tensor": to} if j == 0 else {"expert": plane(j), "tensor": to},
        )

    sent = []

    def dispatch(which, moves, to):
        for k, j, base in moves:
            if j != 0:
                copy = send(which, k, j, base, to, False)
                copy.start()
                sent.append(copy)
                continue

            @pl.when(core == to)
            def _():
                send(which, k, j, base, to, True).start()

            @pl.when(core != to)
            def _():
                send(which, k, j, base, to, False).start()

    def collect(which, moves, me):
        incoming = buffers[which][1]
        for k, j, base in reversed(moves):
            for source in range(2):
                if j == 0 and source == me:
                    send(which, k, j, base, me, True).wait()
                    continue
                here = incoming.at[base + source]
                remote(
                    here, here, a2a_send.at[which, k], a2a_recv.at[which, base + source], {"tensor": other}
                ).wait_recv()

    swap_f.wait_recv()
    lat = (part_f[mine].astype(F32) + got_f[...].astype(F32)).astype(BF16)
    out_lat[...] = dot(table, lat).astype(BF16).reshape(out_lat.shape)
    dispatch(0, first, 0)
    swap_b.wait_recv()
    back = dot(table, part_b[mine]) + dot(table, got_b[...])
    out_grad[...] = (weight * back).astype(BF16).reshape(out_grad.shape)
    dispatch(1, first, 0)
    dispatch(0, second, 0)
    dispatch(1, second, 0)
    dispatch(0, single, 1)
    dispatch(1, single, 1)

    per_sum = len(SUM_PARTS) * 8
    sums = [PlaneSum(more[i * per_sum : (i + 1) * per_sum], xs, ys) for i in range(2)]
    gather = more[2 * per_sum :]

    def expert(moves, me, start, blocks, weight_up, weight_down, summed):
        block = pl.ds(start, blocks)
        rows = pl.ds(start * cap, blocks * cap)
        collect(0, moves, me)
        lat_rows = in_lat[block].reshape(-1, width)
        positive = jnp.maximum(dot(lat_rows, weight_up), 0.0)
        act_ref[rows] = (positive * positive).astype(BF16)
        collect(1, moves, me)
        grad_rows = in_grad[block].reshape(-1, width)
        hidden_grad = dot(grad_rows, weight_down, ((1,), (1,)))
        pre_grad_ref[rows] = (hidden_grad * 2.0 * positive).astype(BF16)
        for j in range(0, width, step):
            piece = dot(act_ref[rows], grad_rows[:, j : j + step], ((0,), (0,)))
            piece = piece.astype(BF16).reshape(ny, nx, dn_rows, step)
            for xx in range(nx):
                summed.down.chunk[xx, :, :, j : j + step] = piece[:, xx]
        summed.down.start()
        cut = min(step, hidden)
        for j in range(0, hidden, cut):
            piece = dot(lat_rows, pre_grad_ref[rows, j : j + cut], ((0,), (0,)))
            piece = piece.astype(BF16).reshape(ny, nx, 2, dn_rows, cut)
            for xx in range(nx):
                summed.up0.chunk[xx, :, :, j : j + cut] = piece[:, xx, 0]
            summed.up1.chunk[:, :, :, j : j + cut] = piece[:, :, 1]
        summed.up1.start()
        summed.up0.start()

    def finish(down_sum, up0_sum, up1_sum):
        gdn_ref[0] = down_sum
        gup_ref[0, 0:dn_rows, :] = up0_sum
        gup_ref[0, dn_rows : 2 * dn_rows, :] = up1_sum

    def sent_within(to, moves):
        for k, j, base in moves:
            if j == 0:
                for which in range(2):
                    send(which, k, j, base, to, False).wait_send()

    @pl.when(core == 0)
    def _():
        up0, up1 = pl.ds(0, dn_rows), pl.ds(dn_rows, dn_rows)
        g = [gather[2 * i : 2 * i + 2] for i in range(6)]
        for copy in slices:
            copy.wait_recv()
        a1 = Direct(lambda t: wdn2.at[y, x], lambda s, k: wdn2.at[s, x], g[0], y, ny, ys.device)
        b1 = Direct(lambda t: wup2.at[y, x, up1], lambda s, k: wup2.at[y, s, up1], g[2], x, nx, xs.device)
        c1 = Direct(lambda t: wup2.at[y, x, up0], lambda s, k: wup2.at[s, x, up0], g[1], y, ny, ys.device)
        b1.wait()
        b2 = Direct(lambda t: wup2.at[y, :, up1], lambda s, k: wup2.at[s, :, up1], g[5], y, ny, ys.device)
        a1.wait()
        a2 = Direct(lambda t: wdn2.at[:, x], lambda s, k: wdn2.at[:, s], g[3], x, nx, xs.device)
        c1.wait()
        c2 = Direct(lambda t: wup2.at[:, x, up0], lambda s, k: wup2.at[:, s, up0], g[4], x, nx, xs.device)

        home, away = sums
        loads[4].wait()
        loads[5].wait()
        expert(first, 0, second_blocks, first_blocks, wup[...], wdn[...], home)
        for part in (a2, b2, c2):
            part.wait()
        expert(
            second, 0, 0, second_blocks,
            wup2[...].reshape(width, hidden), wdn2[...].reshape(hidden, width), away,
        )
        for summed in (home, away):
            summed.down.turn()
            summed.up1.turn()
            summed.up0.turn()
        far_out[0, :, :width] = away.down.total().astype(BF16)
        far_out[0, :, width : width + hidden] = away.up0.total().astype(BF16)
        far_out[0, :, width + hidden :] = away.up1.total().astype(BF16)
        back_home = remote(far_out, far_in, far_send, far_recv, {"expert": far_z})
        back_home.start()
        totals = [home.down.total(), home.up0.total(), home.up1.total()]
        back_home.wait_recv()
        finish(
            totals[0] + far_in[0, :, :width].astype(F32),
            totals[1] + far_in[0, :, width : width + hidden].astype(F32),
            totals[2] + far_in[0, :, width + hidden :].astype(F32),
        )
        sent_within(1, single)
        for copy in slices + [back_home] + home.sent() + away.sent():
            copy.wait_send()
        for part in (a1, b1, c1, a2, b2, c2):
            for copy in part.sent:
                copy.wait_send()

    @pl.when(core == 1)
    def _():
        loads[4].wait()
        loads[5].wait()
        summed = sums[0]
        expert(single, 1, 0, 2 * nz, wup[...], wdn[...], summed)
        summed.down.turn()
        summed.up1.turn()
        summed.up0.turn()
        finish(summed.down.total(), summed.up0.total(), summed.up1.total())
        sent_within(0, first + second)
        for copy in summed.sent():
            copy.wait_send()

    for copy in [swap_f, swap_b] + sent:
        copy.wait_send()


SUM_PARTS = ("down", "up0", "up1")


def shards(ny, nx, tokens, cotangent, latent_down, latent_up, expert_up, expert_down, routes, combine):
    nz = lax.axis_size("expert")
    tok_dev, top = routes.shape
    width, hidden = expert_up.shape[1:]
    experts = 2 * nz
    cap = max(2, 3 * tok_dev * top // (2 * experts))
    rows = hidden // (ny * nx)
    assert width == 2 * hidden

    def sems(*shape):
        return pltpu.SemaphoreType.DMA(shape)

    vmem = pltpu.VMEM
    any_spec = pl.BlockSpec(memory_space=pl.ANY)
    vmem_spec = pl.BlockSpec(memory_space=pltpu.VMEM)

    def two_step(n1, n2, columns):
        return [
            vmem((n1, n2, rows, columns), BF16), vmem((n1, n2, rows, columns), BF16),
            vmem((n2, rows, columns), BF16), vmem((n2, rows, columns), BF16),
            sems(n1), sems(n1), sems(n2), sems(n2),
        ]

    plane_sum = two_step(nx, ny, width) + two_step(nx, ny, hidden) + two_step(ny, nx, hidden)
    gather = [sems(n) for n in (ny, ny, ny, ny, nx, nx, nx, nx, nx, nx, ny, ny)]
    return pl.pallas_call(
        functools.partial(layer, ny, nx, nz, cap),
        out_shape=(
            jax.ShapeDtypeStruct((1, width // (ny * nx), hidden), F32),
            jax.ShapeDtypeStruct((1, rows, width), F32),
        ),
        in_specs=[any_spec] * 6 + [vmem_spec] * 2,
        out_specs=(vmem_spec, vmem_spec),
        scratch_shapes=[
            vmem(tokens.shape, BF16), vmem(cotangent.shape, BF16),
            vmem(latent_down.shape, BF16), vmem(latent_up.shape, BF16),
            vmem((width, hidden), BF16), vmem((hidden, width), BF16), sems(6),
            vmem((2 * tok_dev, width), BF16), vmem((2 * tok_dev, width), BF16),
            vmem((tok_dev, width), BF16), vmem((tok_dev, width), BF16), sems(2), sems(2),
            vmem((experts, cap, width), BF16), vmem((experts, cap, width), BF16),
            vmem((experts, cap, width), BF16), vmem((experts, cap, width), BF16),
            sems(2, experts), sems(2, experts), sems(2, 2),
            vmem((ny, nx, 2 * rows, hidden), BF16), vmem((ny, nx, rows, width), BF16), sems(2), sems(2),
            vmem((experts * cap, hidden), BF16), vmem((experts * cap, hidden), BF16),
            vmem((1, rows, 2 * width), BF16), vmem((1, rows, 2 * width), BF16),
            pltpu.SemaphoreType.DMA, pltpu.SemaphoreType.DMA,
        ]
        + plane_sum
        + plane_sum
        + gather,
        compiler_params=pltpu.CompilerParams(
            collective_id=0, has_side_effects=True, vmem_limit_bytes=56 * 1024 * 1024
        ),
        cost_estimate=pl.CostEstimate(flops=4 * 10**9, bytes_accessed=13 * 10**6, transcendentals=0),
    )(tokens, cotangent, latent_down, latent_up, expert_up, expert_down, routes.T, combine.T)


def solution(mesh):
    return jax.shard_map(
        functools.partial(shards, NY, NX),
        mesh=mesh,
        in_specs=(
            P(("dp", "expert"), "tensor"),
            P(("dp", "expert"), "tensor"),
            P("tensor", None),
            P(None, "tensor"),
            P(("expert", "tensor"), None, None),
            P(("expert", "tensor"), None, None),
            P(("dp", "expert", "tensor"), None),
            P(("dp", "expert", "tensor"), None),
        ),
        out_specs=(P(("expert", "tensor"), "dp", None), P(("expert", "tensor"), "dp", None)),
        check_vma=False,
    )
```

time: 108 us -> 90 us (0.83)
  Pallas kernels: 104 us -> 86.2 us
    pallas_call x1, Pallas kernels: 104 us -> 86.2 us  [shards(): pl.pallas_call(functools.partial(layer, ny, nx, nz, cap), out_shape=(jax....]
where the time goes in v2:
time: 90 us; the launch traced here: 89.8 us
  Pallas kernels  86.2 us (96%)
  local copies, waits for them, and re-layouts  2.95 us (3%)
    pallas_call x1, Pallas kernels, shards(): pl.pallas_call(functools.partial(layer, ny, nx, nz, cap), out_shape=(jax....  86.2 us
    unnamed x2, local copies, waits for them, and re-layouts  2.95 us

profile of v2, /device:TPU:1, one launch (start us, length us, event | category | flops | bytes accessed | tf_op | source)
XLA Modules:
  0.0 89.8 jit_solution(16767393212239732927)
XLA Ops:
  0.6 86.2 %shard_map.95 = (f32[1,32,512]{2,1,0:T(8,128)}, f32[1,16,1024]{2,1,0:T(8,128)}) custom-call(bf16[256,2048]{1,0:T(8,128)(2,1)} %tok_hbm.1, bf16[256,2048]{1,0:T(8,128)(2,1)} %cot_hbm.1, bf16[2048,1024]{1,0:T(8,128)(2,1)} %down_hbm.1, bf16[1024,2048]{1,0:T(8,128)(2,1)} %up_hbm.1, bf16[1,1024,512]{2,1,0:T(8,128)(2,1)} %wup_hbm.1, ...), custom_call_target="tpu_custom_call" | custom-call | flops 4000000000 | bytes 13000000 | tf_op jit(solution)/shard_map/pallas_call | solution.py:417
  86.8 1.5 %copy.12 = f32[1,32,512]{2,1,0:T(8,128)} copy(f32[1,32,512]{2,1,0:T(8,128)} %get-tuple-element.4) | data formatting | bytes 131072
  88.3 1.5 %copy.13 = f32[1,16,1024]{2,1,0:T(8,128)} copy(f32[1,16,1024]{2,1,0:T(8,128)} %get-tuple-element.5) | data formatting | bytes 131072

commit v3 on v2

--- a/solution.py
+++ b/solution.py
@@ -67,14 +67,17 @@
 
     def turn(self):
         self.step1.wait()
-        total = self.chunk[self.first.me].astype(F32)
-        for k in range(1, self.first.n):
-            total = total + self.land[k].astype(F32)
-        self.next[...] = total.astype(BF16)
         r = self.second
-        self.step2 = Direct(
-            lambda t: self.next.at[t], lambda s, k: self.got.at[k], self.sems2, r.me, r.n, r.device
-        )
+
+        def ready(target):
+            total = self.chunk[self.first.me, target].astype(F32)
+            for k in range(1, self.first.n):
+                total = total + self.land[k, target].astype(F32)
+            self.next[target] = total.astype(BF16)
+            return self.next.at[target]
+
+        self.step2 = Direct(ready, lambda s, k: self.got.at[k], self.sems2, r.me, r.n, r.device)
+        ready(r.me)
 
     def total(self):
         self.step2.wait()
@@ -89,13 +92,20 @@
 
 class PlaneSum:
     def __init__(self, refs, xs, ys):
-        n = len(refs) // 3
-        self.down = TwoStepSum(refs[:n], xs, ys)
-        self.up0 = TwoStepSum(refs[n : 2 * n], xs, ys)
-        self.up1 = TwoStepSum(refs[2 * n :], ys, xs)
+        n = len(refs) // 4
+        self.down = [TwoStepSum(refs[i * n : (i + 1) * n], xs, ys) for i in (0, 1)]
+        self.up0 = TwoStepSum(refs[2 * n : 3 * n], xs, ys)
+        self.up1 = TwoStepSum(refs[3 * n :], ys, xs)
+
+    def turn(self):
+        for part in self.down + [self.up1, self.up0]:
+            part.turn()
+
+    def totals(self):
+        return [part.total() for part in self.down + [self.up0, self.up1]]
 
     def sent(self):
-        return self.down.sent() + self.up0.sent() + self.up1.sent()
+        return self.down[0].sent() + self.down[1].sent() + self.up0.sent() + self.up1.sent()
 
 
 def layer(
@@ -133,7 +143,7 @@
             [(tok_hbm, tok), (down_hbm, down), (cot_hbm, cot), (up_hbm, up), (wup_hbm.at[0], wup), (wdn_hbm.at[0], wdn)]
         )
     ]
-    for load in loads:
+    for load in loads[:2]:
         load.start()
 
     barrier = pltpu.get_barrier_semaphore()
@@ -152,41 +162,18 @@
     for k in range(1, ny):
         greet(ys.device(lax.rem(y + k, ny)))
 
+    for load in loads[2:]:
+        load.start()
+
     step = min(256, width)
     loads[0].wait()
     loads[1].wait()
     for j in range(0, width, step):
         part_f[:, j : j + step] = dot(tok[...], down[:, j : j + step]).astype(BF16)
-    pl.semaphore_wait(barrier, len(greeted))
-    theirs = pl.ds(pl.multiple_of(other * tok_dev, tok_dev), tok_dev)
-    mine = pl.ds(pl.multiple_of(core * tok_dev, tok_dev), tok_dev)
-    swap_f = remote(part_f.at[theirs], got_f, swap_send.at[0], swap_recv.at[0], {"tensor": other})
-    swap_f.start()
-
-    up_rows, dn_rows = wup2.shape[2], wdn2.shape[2]
-    slices = [
-        remote(
-            wup_hbm.at[0, pl.ds(pl.multiple_of(group * up_rows, up_rows), up_rows)],
-            wup2.at[y, x], slice_send.at[0], slice_recv.at[0], {"expert": far_z},
-        ),
-        remote(
-            wdn_hbm.at[0, pl.ds(pl.multiple_of(group * dn_rows, dn_rows), dn_rows)],
-            wdn2.at[y, x], slice_send.at[1], slice_recv.at[1], {"expert": far_z},
-        ),
-    ]
-
-    @pl.when(core == 0)
-    def _():
-        for copy in slices:
-            copy.start()
-
     loads[2].wait()
     loads[3].wait()
     for j in range(0, width, step):
         part_b[:, j : j + step] = dot(cot[...], up[j : j + step, :], ((1,), (1,))).astype(BF16)
-    swap_b = remote(part_b.at[theirs], got_b, swap_send.at[1], swap_recv.at[1], {"tensor": other})
-    swap_b.start()
-
     before = (
         lax.broadcasted_iota(jnp.int32, (tok_dev, tok_dev), 0)
         < lax.broadcasted_iota(jnp.int32, (tok_dev, tok_dev), 1)
@@ -209,6 +196,31 @@
         )
     table = table.astype(BF16)
 
+    pl.semaphore_wait(barrier, len(greeted))
+    theirs = pl.ds(pl.multiple_of(other * tok_dev, tok_dev), tok_dev)
+    mine = pl.ds(pl.multiple_of(core * tok_dev, tok_dev), tok_dev)
+    swap_f = remote(part_f.at[theirs], got_f, swap_send.at[0], swap_recv.at[0], {"tensor": other})
+    swap_f.start()
+    swap_b = remote(part_b.at[theirs], got_b, swap_send.at[1], swap_recv.at[1], {"tensor": other})
+    swap_b.start()
+
+    up_rows, dn_rows = wup2.shape[2], wdn2.shape[2]
+    slices = [
+        remote(
+            wup_hbm.at[0, pl.ds(pl.multiple_of(group * up_rows, up_rows), up_rows)],
+            wup2.at[y, x], slice_send.at[0], slice_recv.at[0], {"expert": far_z},
+        ),
+        remote(
+            wdn_hbm.at[0, pl.ds(pl.multiple_of(group * dn_rows, dn_rows), dn_rows)],
+            wdn2.at[y, x], slice_send.at[1], slice_recv.at[1], {"expert": far_z},
+        ),
+    ]
+
+    @pl.when(core == 0)
+    def _():
+        for copy in slices:
+            copy.start()
+
     second = [(k, k - far) for k in range(nz) if reach < k < nz - reach]
     first = [(k, k if k <= reach else k - nz) for k in range(nz) if k <= reach or k >= nz - reach]
     second_blocks, first_blocks = 2 * len(second), 2 * len(first)
@@ -277,7 +289,7 @@
     dispatch(0, single, 1)
     dispatch(1, single, 1)
 
-    per_sum = len(SUM_PARTS) * 8
+    per_sum = 4 * 8
     sums = [PlaneSum(more[i * per_sum : (i + 1) * per_sum], xs, ys) for i in range(2)]
     gather = more[2 * per_sum :]
 
@@ -292,13 +304,15 @@
         grad_rows = in_grad[block].reshape(-1, width)
         hidden_grad = dot(grad_rows, weight_down, ((1,), (1,)))
         pre_grad_ref[rows] = (hidden_grad * 2.0 * positive).astype(BF16)
-        for j in range(0, width, step):
-            piece = dot(act_ref[rows], grad_rows[:, j : j + step], ((0,), (0,)))
-            piece = piece.astype(BF16).reshape(ny, nx, dn_rows, step)
+        cut = min(step, hidden)
+        for j in range(0, width, cut):
+            piece = dot(act_ref[rows], grad_rows[:, j : j + cut], ((0,), (0,)))
+            piece = piece.astype(BF16).reshape(ny, nx, dn_rows, cut)
+            part, at = summed.down[j // hidden], j % hidden
             for xx in range(nx):
-                summed.down.chunk[xx, :, :, j : j + step] = piece[:, xx]
-        summed.down.start()
-        cut = min(step, hidden)
+                part.chunk[xx, :, :, at : at + cut] = piece[:, xx]
+            if at + cut == hidden:
+                part.start()
         for j in range(0, hidden, cut):
             piece = dot(lat_rows, pre_grad_ref[rows, j : j + cut], ((0,), (0,)))
             piece = piece.astype(BF16).reshape(ny, nx, 2, dn_rows, cut)
@@ -308,10 +322,10 @@
         summed.up1.start()
         summed.up0.start()
 
-    def finish(down_sum, up0_sum, up1_sum):
-        gdn_ref[0] = down_sum
-        gup_ref[0, 0:dn_rows, :] = up0_sum
-        gup_ref[0, dn_rows : 2 * dn_rows, :] = up1_sum
+    def finish(totals):
+        for i in range(2):
+            gdn_ref[0, :, i * hidden : (i + 1) * hidden] = totals[i]
+            gup_ref[0, i * dn_rows : (i + 1) * dn_rows, :] = totals[2 + i]
 
     def sent_within(to, moves):
         for k, j, base in moves:
@@ -345,22 +359,18 @@
             second, 0, 0, second_blocks,
             wup2[...].reshape(width, hidden), wdn2[...].reshape(hidden, width), away,
         )
-        for summed in (home, away):
-            summed.down.turn()
-            summed.up1.turn()
-            summed.up0.turn()
-        far_out[0, :, :width] = away.down.total().astype(BF16)
-        far_out[0, :, width : width + hidden] = away.up0.total().astype(BF16)
-        far_out[0, :, width + hidden :] = away.up1.total().astype(BF16)
+        home.turn()
+        away.turn()
+        for i, part in enumerate(away.totals()):
+            far_out[0, :, i * hidden : (i + 1) * hidden] = part.astype(BF16)
         back_home = remote(far_out, far_in, far_send, far_recv, {"expert": far_z})
         back_home.start()
-        totals = [home.down.total(), home.up0.total(), home.up1.total()]
+        totals = home.totals()
         back_home.wait_recv()
-        finish(
-            totals[0] + far_in[0, :, :width].astype(F32),
-            totals[1] + far_in[0, :, width : width + hidden].astype(F32),
-            totals[2] + far_in[0, :, width + hidden :].astype(F32),
-        )
+        finish([
+            part + far_in[0, :, i * hidden : (i + 1) * hidden].astype(F32)
+            for i, part in enumerate(totals)
+        ])
         sent_within(1, single)
         for copy in slices + [back_home] + home.sent() + away.sent():
             copy.wait_send()
@@ -374,19 +384,14 @@
         loads[5].wait()
         summed = sums[0]
         expert(single, 1, 0, 2 * nz, wup[...], wdn[...], summed)
-        summed.down.turn()
-        summed.up1.turn()
-        summed.up0.turn()
-        finish(summed.down.total(), summed.up0.total(), summed.up1.total())
+        summed.turn()
+        finish(summed.totals())
         sent_within(0, first + second)
         for copy in summed.sent():
             copy.wait_send()
 
     for copy in [swap_f, swap_b] + sent:
         copy.wait_send()
-
-
-SUM_PARTS = ("down", "up0", "up1")
 
 
 def shards(ny, nx, tokens, cotangent, latent_down, latent_up, expert_up, expert_down, routes, combine):
@@ -412,7 +417,7 @@
             sems(n1), sems(n1), sems(n2), sems(n2),
         ]
 
-    plane_sum = two_step(nx, ny, width) + two_step(nx, ny, hidden) + two_step(ny, nx, hidden)
+    plane_sum = 3 * two_step(nx, ny, hidden) + two_step(ny, nx, hidden)
     gather = [sems(n) for n in (ny, ny, ny, ny, nx, nx, nx, nx, nx, nx, ny, ny)]
     return pl.pallas_call(
         functools.partial(layer, ny, nx, nz, cap),

time: 90 us -> 91.7 us (1.019)
  Pallas kernels: 86.2 us -> 87.9 us
    pallas_call x1, Pallas kernels: 86.2 us -> 87.9 us  [shards(): pl.pallas_call(functools.partial(layer, ny, nx, nz, cap), out_shape=(jax....]
where the time goes in v3:
time: 91.7 us; the launch traced here: 91.4 us
  Pallas kernels  87.9 us (96%)
  local copies, waits for them, and re-layouts  2.95 us (3%)
    pallas_call x1, Pallas kernels, shards(): pl.pallas_call(functools.partial(layer, ny, nx, nz, cap), out_shape=(jax....  87.9 us
    unnamed x2, local copies, waits for them, and re-layouts  2.95 us

profile of v3, /device:TPU:1, one launch (start us, length us, event | category | flops | bytes accessed | tf_op | source)
XLA Modules:
  0.0 91.4 jit_solution(5148410602211849193)
XLA Ops:
  0.6 87.9 %shard_map.95 = (f32[1,32,512]{2,1,0:T(8,128)}, f32[1,16,1024]{2,1,0:T(8,128)}) custom-call(bf16[256,2048]{1,0:T(8,128)(2,1)} %tok_hbm.1, bf16[256,2048]{1,0:T(8,128)(2,1)} %cot_hbm.1, bf16[2048,1024]{1,0:T(8,128)(2,1)} %down_hbm.1, bf16[1024,2048]{1,0:T(8,128)(2,1)} %up_hbm.1, bf16[1,1024,512]{2,1,0:T(8,128)(2,1)} %wup_hbm.1, ...), custom_call_target="tpu_custom_call" | custom-call | flops 4000000000 | bytes 13000000 | tf_op jit(solution)/shard_map/pallas_call | solution.py:422
  88.5 1.5 %copy.12 = f32[1,32,512]{2,1,0:T(8,128)} copy(f32[1,32,512]{2,1,0:T(8,128)} %get-tuple-element.4) | data formatting | bytes 131072
  90.0 1.5 %copy.13 = f32[1,16,1024]{2,1,0:T(8,128)} copy(f32[1,16,1024]{2,1,0:T(8,128)} %get-tuple-element.5) | data formatting | bytes 131072

commit v4 on v2

--- a/solution.py
+++ b/solution.py
@@ -67,14 +67,17 @@
 
     def turn(self):
         self.step1.wait()
-        total = self.chunk[self.first.me].astype(F32)
-        for k in range(1, self.first.n):
-            total = total + self.land[k].astype(F32)
-        self.next[...] = total.astype(BF16)
         r = self.second
-        self.step2 = Direct(
-            lambda t: self.next.at[t], lambda s, k: self.got.at[k], self.sems2, r.me, r.n, r.device
-        )
+
+        def ready(target):
+            total = self.chunk[self.first.me, target].astype(F32)
+            for k in range(1, self.first.n):
+                total = total + self.land[k, target].astype(F32)
+            self.next[target] = total.astype(BF16)
+            return self.next.at[target]
+
+        self.step2 = Direct(ready, lambda s, k: self.got.at[k], self.sems2, r.me, r.n, r.device)
+        ready(r.me)
 
     def total(self):
         self.step2.wait()
@@ -93,6 +96,11 @@
         self.down = TwoStepSum(refs[:n], xs, ys)
         self.up0 = TwoStepSum(refs[n : 2 * n], xs, ys)
         self.up1 = TwoStepSum(refs[2 * n :], ys, xs)
+
+    def totals(self):
+        down, up0, up1 = self.down.total(), self.up0.total(), self.up1.total()
+        hidden = up0.shape[1]
+        return jnp.concatenate([down, up1[:, hidden:]], axis=1), up0, up1[:, :hidden]
 
     def sent(self):
         return self.down.sent() + self.up0.sent() + self.up1.sent()
@@ -292,11 +300,15 @@
         grad_rows = in_grad[block].reshape(-1, width)
         hidden_grad = dot(grad_rows, weight_down, ((1,), (1,)))
         pre_grad_ref[rows] = (hidden_grad * 2.0 * positive).astype(BF16)
+        main = width - width // 8
         for j in range(0, width, step):
             piece = dot(act_ref[rows], grad_rows[:, j : j + step], ((0,), (0,)))
             piece = piece.astype(BF16).reshape(ny, nx, dn_rows, step)
+            stop = min(j + step, main)
             for xx in range(nx):
-                summed.down.chunk[xx, :, :, j : j + step] = piece[:, xx]
+                summed.down.chunk[xx, :, :, j:stop] = piece[:, xx, :, : stop - j]
+            if stop < j + step:
+                summed.up1.chunk[:, :, :, hidden + stop - main : hidden + j + step - main] = piece[..., stop - j :]
         summed.down.start()
         cut = min(step, hidden)
         for j in range(0, hidden, cut):
@@ -349,12 +361,13 @@
             summed.down.turn()
             summed.up1.turn()
             summed.up0.turn()
-        far_out[0, :, :width] = away.down.total().astype(BF16)
-        far_out[0, :, width : width + hidden] = away.up0.total().astype(BF16)
-        far_out[0, :, width + hidden :] = away.up1.total().astype(BF16)
+        down_sum, up0_sum, up1_sum = away.totals()
+        far_out[0, :, :width] = down_sum.astype(BF16)
+        far_out[0, :, width : width + hidden] = up0_sum.astype(BF16)
+        far_out[0, :, width + hidden :] = up1_sum.astype(BF16)
         back_home = remote(far_out, far_in, far_send, far_recv, {"expert": far_z})
         back_home.start()
-        totals = [home.down.total(), home.up0.total(), home.up1.total()]
+        totals = home.totals()
         back_home.wait_recv()
         finish(
             totals[0] + far_in[0, :, :width].astype(F32),
@@ -377,7 +390,7 @@
         summed.down.turn()
         summed.up1.turn()
         summed.up0.turn()
-        finish(summed.down.total(), summed.up0.total(), summed.up1.total())
+        finish(*summed.totals())
         sent_within(0, first + second)
         for copy in summed.sent():
             copy.wait_send()
@@ -412,7 +425,11 @@
             sems(n1), sems(n1), sems(n2), sems(n2),
         ]
 
-    plane_sum = two_step(nx, ny, width) + two_step(nx, ny, hidden) + two_step(ny, nx, hidden)
+    plane_sum = (
+        two_step(nx, ny, width - width // 8)
+        + two_step(nx, ny, hidden)
+        + two_step(ny, nx, hidden + width // 8)
+    )
     gather = [sems(n) for n in (ny, ny, ny, ny, nx, nx, nx, nx, nx, nx, ny, ny)]
     return pl.pallas_call(
         functools.partial(layer, ny, nx, nz, cap),

time: 90 us -> 89 us (0.989)
  Pallas kernels: 86.2 us -> 85.2 us
    pallas_call x1, Pallas kernels: 86.2 us -> 85.2 us  [shards(): pl.pallas_call(functools.partial(layer, ny, nx, nz, cap), out_shape=(jax....]
where the time goes in v4:
time: 89 us; the launch traced here: 88.8 us
  Pallas kernels  85.2 us (96%)
  local copies, waits for them, and re-layouts  2.95 us (3%)
    pallas_call x1, Pallas kernels, shards(): pl.pallas_call(functools.partial(layer, ny, nx, nz, cap), out_shape=(jax....  85.2 us
    unnamed x2, local copies, waits for them, and re-layouts  2.95 us

profile of v4, /device:TPU:1, one launch (start us, length us, event | category | flops | bytes accessed | tf_op | source)
XLA Modules:
  0.0 88.8 jit_solution(3056637510160030985)
XLA Ops:
  0.6 85.2 %shard_map.95 = (f32[1,32,512]{2,1,0:T(8,128)}, f32[1,16,1024]{2,1,0:T(8,128)}) custom-call(bf16[256,2048]{1,0:T(8,128)(2,1)} %tok_hbm.1, bf16[256,2048]{1,0:T(8,128)(2,1)} %cot_hbm.1, bf16[2048,1024]{1,0:T(8,128)(2,1)} %down_hbm.1, bf16[1024,2048]{1,0:T(8,128)(2,1)} %up_hbm.1, bf16[1,1024,512]{2,1,0:T(8,128)(2,1)} %wup_hbm.1, ...), custom_call_target="tpu_custom_call" | custom-call | flops 4000000000 | bytes 13000000 | tf_op jit(solution)/shard_map/pallas_call | solution.py:434
  85.8 1.5 %copy.12 = f32[1,32,512]{2,1,0:T(8,128)} copy(f32[1,32,512]{2,1,0:T(8,128)} %get-tuple-element.4) | data formatting | bytes 131072
  87.3 1.5 %copy.13 = f32[1,16,1024]{2,1,0:T(8,128)} copy(f32[1,16,1024]{2,1,0:T(8,128)} %get-tuple-element.5) | data formatting | bytes 131072
